TPU v7x, 32 devices: a whole 2x2x4 slice. The times are simulated.
32 devices in a mesh: group: 4 (over x, core), inner: 8 (over z, y).
Axes of the slice: x: 2, y: 2, z: 4, core: 2. Of those that a mesh axis runs over, the one named last changes fastest.
Arguments:
- out_grad: bfloat16 [64, 3584], P(('group', 'inner')), may hold values from -6 to 6
- routing_weight: bfloat16 [64, 4], P(('group', 'inner')), may hold values from 0.099609375 to 1
- expert_ids: int32 [64, 4], P(('group', 'inner')), may hold values from 0 to 15, as said below
- slot_index: int32 [64, 4], P(('group', 'inner')), may hold values from 0 to 5, as said below
- w_gate: bfloat16 [3584, 4096], P(None, ('group', 'inner')), may hold values from -0.09375 to 0.09375
- w_up: bfloat16 [3584, 4096], P(None, ('group', 'inner')), may hold values from -0.09375 to 0.09375
- w_down: bfloat16 [4096, 3584], P(('group', 'inner')), may hold values from -0.375 to 0.375
- pre_act: bfloat16 [2, 24, 4096], P(None, None, ('group', 'inner')), may hold values from -5 to 5
Outputs:
- grad_tokens: bfloat16 [64, 3584], P(('group', 'inner'))
- grad_routing: float32 [64, 4], P(('group', 'inner'))
Inputs may be any that keep to these rules, and one draw needn't show every extreme that they name: `expert_ids`: each token names 4 different experts, two in each of 2 different node groups (expert e lies in group e // 4). Among the 16 tokens of one index of group, every node group is named by exactly half of the tokens, and in every node group half of the experts are named by exactly 6 of these tokens and the other half by 2. slot_index[t, k] is the number of tokens before t, among the 16 tokens of the same index of group, that name expert expert_ids[t, k].
All inputs are finite; a program needn't handle non-finite values.
Results may differ from a plain program's by a relative error of at most 0.0075.
Values may be sent and summed in bfloat16 or wider, within the bound.
No kernel may reach another device: no remote copies, remote signals or barrier semaphores. Data moves between devices by JAX's collectives and lax.ppermute only.
A program may use at most 64 MiB of HBM per device.

v0:
```python
import functools

import jax
import jax.numpy as jnp
from jax import lax
from jax.experimental import pallas as pl
from jax.experimental.pallas import tpu as pltpu
from jax.sharding import Mesh, PartitionSpec as P

LANES = 128
CORES = 2
SAVED_ROWS = 32


def exchange(array, axis):
    return lax.all_to_all(array, axis, split_axis=0, concat_axis=0, tiled=True)


def pack(rows, *small):
    width = sum(s.shape[1] for s in small)
    fill = jnp.zeros((rows.shape[0], -width % LANES), rows.dtype)
    return jnp.concatenate([rows, *(s.astype(rows.dtype) for s in small), fill], axis=1)


def gradients(back_proj, weight, pre_gate, pre_up):
    gate_sig = jax.nn.sigmoid(pre_gate)
    swish_gate = pre_gate * gate_sig
    gate_piece = jnp.sum(swish_gate * pre_up * back_proj, axis=1, keepdims=True)
    scaled = weight * back_proj
    grad_up = (scaled * swish_gate).astype(jnp.bfloat16)
    grad_gate = (scaled * pre_up * gate_sig * (1.0 + pre_gate * (1.0 - gate_sig))).astype(
        jnp.bfloat16
    )
    return grad_gate, grad_up, gate_piece


def across(a, b):
    return lax.dot_general(a, b, (((1,), (1,)), ((), ())), preferred_element_type=jnp.float32)


def sizes(group_count, inner_count):
    split_count = min(8, inner_count // 4)
    return split_count, inner_count // split_count


def pack_kernel(
    out_grad, ids, slots, weights, w_gate, w_up, w_down, pre_act,
    sent, both, rows, words, reals, saved, small, sems,
):
    width, topk = w_gate.shape[0], ids.shape[1]
    first_down = 2 * width + 2 * SAVED_ROWS
    copies = [
        pltpu.make_async_copy(source, target, sems.at[at])
        for at, (source, target) in enumerate(
            (
                (ids, words.at[0]),
                (slots, words.at[1]),
                (weights, reals),
                (out_grad, rows),
                (pre_act, saved),
                (w_gate, both.at[:width]),
                (w_up, both.at[width : 2 * width]),
                *(
                    (w_down.at[:, at : at + LANES], both.at[first_down + at : first_down + at + LANES])
                    for at in range(0, width, LANES)
                ),
            )
        )
    ]
    for copy in copies:
        copy.start()
    small[...] = jnp.zeros_like(small)
    both[2 * width : first_down] = jnp.zeros((2 * SAVED_ROWS, LANES), both.dtype)
    for copy in copies[:5]:
        copy.wait()
    for at, part in enumerate((words[0], words[1], reals[...])):
        small[:, at * topk : (at + 1) * topk] = part.astype(jnp.float32)
    tail = small[...].astype(sent.dtype)
    own_rows = rows[...]
    for peer in range(sent.shape[0]):
        sent[peer, :, :width] = own_rows
        sent[peer, :, width:] = tail
    for at in range(2):
        first = 2 * width + at * SAVED_ROWS
        both[first : first + saved.shape[1]] = saved[at]
    for copy in copies[5:]:
        copy.wait()


def expert_kernel(own_rows, topk, slots, *refs):
    arrived, outs = refs[:own_rows], refs[own_rows + 2 :]
    both1, both2 = refs[own_rows : own_rows + 2]
    half, width = own_rows * arrived[0].shape[0], arrived[0].shape[1] - LANES
    row_count = lax.axis_size("row")
    peers = row_count * lax.axis_size("inner")
    capacity = slots // (row_count * CORES)
    split_count, experts_here = sizes(row_count * CORES, lax.axis_size("inner"))
    core = lax.axis_index("core")
    group_row = lax.axis_index("row") * CORES
    local_expert = lax.axis_index("inner") // split_count
    small = jnp.concatenate([part[:, width:] for part in arrived]).astype(jnp.float32)
    lane = lax.broadcasted_iota(jnp.int32, small.shape, 1)
    peer = lax.broadcasted_iota(jnp.int32, (half, slots), 0) % peers
    source = peer // (peers // row_count)
    first = (source * CORES + core) * capacity
    column = lax.broadcasted_iota(jnp.int32, (half, slots), 1)

    def routed(group_core):
        expert = (group_row + group_core) * experts_here + local_expert
        mine = jnp.where(
            jnp.logical_and(small == expert.astype(jnp.float32), lane < topk), 1.0, 0.0
        )
        slot = jnp.sum(pltpu.roll(mine, topk, 1) * small, axis=1, keepdims=True)
        weight = jnp.sum(pltpu.roll(mine, 2 * topk, 1) * small, axis=1, keepdims=True)
        chosen = jnp.sum(mine, axis=1, keepdims=True)
        hit = jnp.logical_and(first + slot.astype(jnp.int32) == column, chosen > 0.5)
        return mine, weight, jnp.where(hit, 1.0, 0.0).astype(jnp.bfloat16)

    def backward(routing, back_proj, both):
        mine, weight, one_hot = routing
        pre_gate, pre_up = [
            jnp.dot(
                one_hot,
                both[2 * width + at * SAVED_ROWS : 2 * width + at * SAVED_ROWS + slots],
                preferred_element_type=jnp.float32,
            )
            for at in range(2)
        ]
        grad_gate, grad_up, gate_piece = gradients(back_proj, weight, pre_gate, pre_up)
        return grad_gate, grad_up, mine * gate_piece

    def store(cols, values):
        for at, out in enumerate(outs):
            out[:, cols] = values[at * peers : (at + 1) * peers].astype(out.dtype)

    def back(both):
        first = 2 * width + 2 * SAVED_ROWS
        blocks = [both[first + at : first + at + LANES] for at in range(0, width, LANES)]
        return across(rows, jnp.concatenate(blocks, axis=1))

    rows = jnp.concatenate([part[:, :width] for part in arrived])
    own, other = routed(core), routed(1 - core)
    grad_gate1, grad_up1, gates1 = backward(own, back(both1), both1)
    grad_gate2, grad_up2, gates2 = backward(other, back(both2), both2)
    grads = jnp.concatenate([grad_gate1, grad_up1, grad_gate2, grad_up2], axis=1)
    step = 512 if width % 512 == 0 else LANES
    for at in range(0, width, step):
        weights = [b[first + at : first + at + step] for b in (both1, both2) for first in (0, width)]
        store(slice(at, at + step), across(grads, jnp.concatenate(weights, axis=1)))
    store(slice(width, width + LANES), gates1 + gates2)


def stay_in(space, *arrays):
    return [pltpu.with_memory_space_constraint(a, space) for a in arrays]


def swap_cores(array):
    return lax.ppermute(array, "core", [(0, 1), (1, 0)])


def flat(out_grad, routing_weight, expert_ids, slot_index, w_gate, w_up, w_down, pre_act):
    row_count = lax.axis_size("row")
    inner_count = lax.axis_size("inner")
    own, width = out_grad.shape
    topk = expert_ids.shape[1]
    peers = row_count * inner_count
    half = peers * own
    slots, hidden = pre_act.shape[1:]
    packed = width + LANES
    in_vmem = pl.BlockSpec(memory_space=pltpu.VMEM)
    in_hbm = pl.BlockSpec(memory_space=pltpu.HBM)
    bf16 = out_grad.dtype

    sent, both = pl.pallas_call(
        pack_kernel,
        out_shape=[
            jax.ShapeDtypeStruct((peers, own, packed), bf16),
            pltpu.VMEM((3 * width + 2 * SAVED_ROWS, hidden), bf16),
        ],
        in_specs=[in_hbm] * 8,
        out_specs=[in_vmem] * 2,
        scratch_shapes=[
            pltpu.VMEM((own, width), bf16),
            pltpu.VMEM((2, own, topk), expert_ids.dtype),
            pltpu.VMEM((own, topk), bf16),
            pltpu.VMEM(pre_act.shape, bf16),
            pltpu.VMEM((own, LANES), jnp.float32),
            pltpu.SemaphoreType.DMA((7 + width // LANES,)),
        ],
        compiler_params=pltpu.CompilerParams(vmem_limit_bytes=16 * 2**20),
        name="pack_rows",
    )(
        *stay_in(
            pltpu.HBM,
            *(out_grad, expert_ids, slot_index, routing_weight),
            *(w_gate, w_up, w_down, pre_act),
        )
    )
    both2 = swap_cores(both)
    arrived = exchange(sent, ("row", "inner"))
    pieces = pl.pallas_call(
        functools.partial(expert_kernel, own, topk, slots),
        out_shape=[jax.ShapeDtypeStruct((peers, packed), bf16)] * own,
        in_specs=[in_vmem] * (own + 2),
        out_specs=[in_vmem] * own,
        compiler_params=pltpu.CompilerParams(vmem_limit_bytes=16 * 2**20),
        cost_estimate=pl.CostEstimate(
            flops=12 * half * w_down.size,
            bytes_accessed=2 * (both.nbytes + arrived.nbytes),
            transcendentals=2 * half * hidden,
        ),
        name="expert_pieces",
    )(
        *(arrived[:, at] for at in range(own)),
        *stay_in(pltpu.VMEM, both, both2),
    )
    returned = exchange(jnp.stack(pieces, axis=1), ("row", "inner"))
    rows, gates = returned[:, :, :width], returned[:, :, width : width + topk]
    grad_rows = jnp.sum(rows.astype(jnp.float32), axis=0).astype(out_grad.dtype)
    return grad_rows, jnp.sum(gates.astype(jnp.float32), axis=0)


def staged(out_grad, routing_weight, expert_ids, slot_index, w_gate, w_up, w_down, pre_act):
    group_count = lax.axis_size("group")
    inner_count = lax.axis_size("inner")
    own, width = out_grad.shape
    topk = expert_ids.shape[1]
    split_count, experts_here = sizes(group_count, inner_count)
    local_expert = lax.axis_index("inner") // split_count
    block = inner_count * own
    slots = pre_act.shape[1]
    capacity = slots // group_count
    high = -(-(capacity + 1) // 8) * 8

    payload = pack(out_grad, expert_ids, slot_index, routing_weight)
    sent = jnp.broadcast_to(payload[None], (inner_count,) + payload.shape)
    arrived = exchange(sent, "inner").reshape(block, payload.shape[1])
    rows = arrived[:, :width]
    small = arrived[:, width : width + 3 * topk].astype(jnp.float32)
    ids = small[:, :topk].astype(jnp.int32)
    slot = small[:, topk : 2 * topk].astype(jnp.int32)
    weight = small[:, 2 * topk :]
    selected = ids % experts_here == local_expert
    column = ids // experts_here * high + slot
    one_hot = jnp.logical_and(
        column[:, :, None] == jnp.arange(group_count * high, dtype=jnp.int32), selected[:, :, None]
    ).astype(jnp.float32)
    placement = jnp.sum(one_hot, axis=1).astype(jnp.bfloat16)
    send_weight = jnp.sum(one_hot * weight[:, :, None], axis=(0, 1)).reshape(group_count, 1, high)
    send_rows = lax.dot_general(
        placement, rows, (((0,), (0,)), ((), ())), preferred_element_type=jnp.float32
    ).reshape(group_count, high, width)
    last = jnp.arange(high) == high - 1
    weight_row = jnp.pad(send_weight, ((0, 0), (0, 0), (0, width - high)))
    send = jnp.where(last[None, :, None], weight_row, send_rows).astype(jnp.bfloat16)
    buffer = exchange(send, "group")

    buffer_weight = buffer[:, high - 1, :capacity].astype(jnp.float32).reshape(slots, 1)
    buffer_rows = buffer[:, :capacity].reshape(slots, width)
    back_proj = across(buffer_rows, w_down)
    grad_gate, grad_up, gate_piece = gradients(
        back_proj, buffer_weight, pre_act[0].astype(jnp.float32), pre_act[1].astype(jnp.float32)
    )
    pieces = (across(grad_gate, w_gate) + across(grad_up, w_up)).reshape(group_count, capacity, width)
    gate_row = jnp.pad(
        gate_piece.reshape(group_count, 1, capacity), ((0, 0), (0, 0), (0, width - capacity))
    )
    pieces = jnp.pad(pieces, ((0, 0), (0, high - capacity), (0, 0)))
    back = exchange(jnp.where(last[None, :, None], gate_row, pieces).astype(jnp.bfloat16), "group")

    owned = jnp.dot(
        placement, back.reshape(group_count * high, width), preferred_element_type=jnp.float32
    ).astype(jnp.bfloat16)
    gates = back[:, high - 1, :high].reshape(group_count * high).astype(jnp.float32)
    gate_rows = jnp.sum(one_hot * gates, axis=2)
    final = exchange(pack(owned, gate_rows).reshape(inner_count, own, -1), "inner")
    total = jnp.sum(final.astype(jnp.float32), axis=0)
    return total[:, :width].astype(jnp.bfloat16), total[:, width : width + topk]


def solution(mesh):
    if mesh.size <= 64:
        group_count, inner_count = mesh.devices.shape
        devices = mesh.devices.reshape(group_count // CORES, CORES, inner_count)
        mesh, axes, on_device = Mesh(devices, ("row", "core", "inner")), ("row", "core", "inner"), flat
    else:
        axes, on_device = ("group", "inner"), staged
    token, hidden = P(axes, None), P(None, axes)
    return jax.shard_map(
        on_device,
        mesh=mesh,
        in_specs=(token, token, token, token, hidden, hidden, token, P(None, None, axes)),
        out_specs=(token, token),
        check_vma=False,
    )
```

profile of v0, /device:TPU:0, one launch (start us, length us, event | category | flops | bytes accessed | tf_op | source)
XLA Modules:
  0.0 36.8 jit_solution(9465378601469151454)
XLA Ops:
  0.6 2.0 %pack_rows.1 = (bf16[16,2,3712]{2,1,0:T(2,128)(2,1)S(1)}, bf16[10816,128]{1,0:T(8,128)(2,1)S(1)}) custom-call(bf16[2,3584]{1,0:T(2,128)(2,1)} %out_grad.1, s32[2,4]{1,0:T(2,128)} %ids.1, s32[2,4]{1,0:T(2,128)} %slots.1, bf16[2,4]{1,0:T(2,128)(2,1)} %weights.1, bf16[3584,128]{1,0:T(8,128)(2,1)} %w_gate.1, bf16[3584,128]{1,0:T(8,128)(2,1)} %w_up.1, ...), custom_call_target="tpu_custom_call" | custom-call | tf_op jit(solution)/shard_map/pack_rows/pallas_call | solution.py:174
  2.6 0.5 %collective-permute-start = (bf16[10816,128]{1,0:T(8,128)(2,1)S(1)}, bf16[10816,128]{1,0:T(8,128)(2,1)S(1)}, u32[]{:S(2)}, u32[]{:S(2)}) collective-permute-start(bf16[10816,128]{1,0:T(8,128)(2,1)S(1)} %get-tuple-element.7.refs_2_), channel_id=1, source_target_pairs={{0,8},{8,0},{1,9},{9,1},{2,10},{10,2},{3,11},{11,3},{4,12},{12,4},... | collective-permute-start | bytes 8306696 | tf_op jit(solution)/shard_map/ppermute | solution.py:158
  3.2 17.7 %all_to_all.10 = bf16[16,2,3712]{2,1,0:T(2,128)(2,1)S(1)} all-to-all(bf16[16,2,3712]{2,1,0:T(2,128)(2,1)S(1)} %get-tuple-element.6), channel_id=1, replica_groups=mesh['row'=2,'core'=2,'inner'=8] {'row','inner'}, dimensions={0} | all-to-all | bytes 475136 | tf_op jit(solution)/shard_map/all_to_all | solution.py:16
  20.9 0.3 fusion
  21.3 0.0 collective-permute-done.refs_3_
  21.3 1.7 %expert_pieces.1 = (bf16[16,3712]{1,0:T(8,128)(2,1)S(1)}, bf16[16,3712]{1,0:T(8,128)(2,1)S(1)}) custom-call(bf16[16,3712]{1,0:T(8,128)(2,1)S(1)} %get-tuple-element.13.refs_0_, bf16[16,3712]{1,0:T(8,128)(2,1)S(1)} %get-tuple-element.12.refs_1_, bf16[10816,128]{1,0:T(8,128)(2,1)S(1)} %get-tuple-element.7.refs_2_, ...), custom_call_target="tpu_custom_call" | custom-call | flops 176160768 | bytes 6012928 | tf_op jit(solution)/shard_map/expert_pieces/pallas_call | solution.py:201
  23.1 0.2 copy.13
  23.2 12.2 %all_to_all.11 = bf16[16,2,3712]{2,1,0:T(2,128)(2,1)S(1)} all-to-all(bf16[16,2,3712]{2,1,0:T(2,128)(2,1)S(1)} %copy.13), channel_id=1, replica_groups=mesh['row'=2,'core'=2,'inner'=8] {'row','inner'}, dimensions={0} | all-to-all | bytes 475136 | tf_op jit(solution)/shard_map/all_to_all | solution.py:16
  35.4 0.6 %convert_reduce_fusion = f32[2,4]{1,0:T(2,128)} fusion(bf16[16,2,3712]{2,1,0:T(2,128)(2,1)S(1)} %all_to_all.11), kind=kLoop, calls=%fused_computation.4 | loop fusion | flops 248 | bytes 288 | tf_op jit(solution)/shard_map/reduce_sum | solution.py:220
  36.0 0.8 %slice_reduce_fusion = bf16[2,3584]{1,0:T(2,128)(2,1)} fusion(bf16[16,2,3712]{2,1,0:T(2,128)(2,1)S(1)} %all_to_all.11), kind=kLoop, calls=%fused_computation.1 | loop fusion | flops 107520 | bytes 243712 | tf_op jit(solution)/shard_map/reduce_sum | solution.py:219
  (2 shorter events, 0.1 us)
Async XLA Ops:
  2.6 18.6 %collective-permute-start = (bf16[10816,128]{1,0:T(8,128)(2,1)S(1)}, bf16[10816,128]{1,0:T(8,128)(2,1)S(1)}, u32[]{:S(2)}, u32[]{:S(2)}) collective-permute-start(bf16[10816,128]{1,0:T(8,128)(2,1)S(1)} %get-tuple-element.7.refs_2_), channel_id=1, source_target_pairs={{0,8},{8,0},{1,9},{9,1},{2,10},{10,2},{3,11},{11,3},{4,12},{12,4},... | collective-permute-start | bytes 8306696 | tf_op jit(solution)/shard_map/ppermute | solution.py:158
where the time goes:
time: 37.1 us; the launch traced here: 36.8 us
  blocking collectives  29.9 us (81%)
  Pallas kernels  3.73 us (10%)
  other arithmetic  1.41 us (4%)
  between operations  0.68 us (2%)
  local copies, waits for them, and re-layouts  0.56 us (2%)
  starting transfers between devices  0.52 us (1%)
    all_to_all x2, blocking collectives, exchange(): return lax.all_to_all(array, axis, split_axis=0, concat_axis=0, tiled=True)  29.9 us
    pallas_call x1, Pallas kernels, flat(): pl.pallas_call(pack_kernel, out_shape=[jax.ShapeDtypeStruct((peers, own,...  1.99 us
    pallas_call x1, Pallas kernels, flat(): pl.pallas_call(functools.partial(expert_kernel, own, topk, slots), out_sh...  1.73 us
    reduce_sum x1, other arithmetic, flat(): grad_rows = jnp.sum(rows.astype(jnp.float32), axis=0).astype(out_grad.dtype)  0.79 us
  transfers between devices with their start and end apart: 1, of which 0 were waited for; matrix products, arithmetic and copies ran while one was open for 1% of the time, Pallas kernels for 0%

commit v1 on v0

--- a/solution.py
+++ b/solution.py
@@ -87,10 +87,8 @@
         copy.wait()
 
 
-def expert_kernel(own_rows, topk, slots, *refs):
-    arrived, outs = refs[:own_rows], refs[own_rows + 2 :]
-    both1, both2 = refs[own_rows : own_rows + 2]
-    half, width = own_rows * arrived[0].shape[0], arrived[0].shape[1] - LANES
+def expert_kernel(topk, slots, arrived, both1, both2, out):
+    half, width = arrived.shape[0], arrived.shape[1] - LANES
     row_count = lax.axis_size("row")
     peers = row_count * lax.axis_size("inner")
     capacity = slots // (row_count * CORES)
@@ -98,7 +96,7 @@
     core = lax.axis_index("core")
     group_row = lax.axis_index("row") * CORES
     local_expert = lax.axis_index("inner") // split_count
-    small = jnp.concatenate([part[:, width:] for part in arrived]).astype(jnp.float32)
+    small = arrived[:, width:].astype(jnp.float32)
     lane = lax.broadcasted_iota(jnp.int32, small.shape, 1)
     peer = lax.broadcasted_iota(jnp.int32, (half, slots), 0) % peers
     source = peer // (peers // row_count)
@@ -129,16 +127,12 @@
         grad_gate, grad_up, gate_piece = gradients(back_proj, weight, pre_gate, pre_up)
         return grad_gate, grad_up, mine * gate_piece
 
-    def store(cols, values):
-        for at, out in enumerate(outs):
-            out[:, cols] = values[at * peers : (at + 1) * peers].astype(out.dtype)
-
     def back(both):
         first = 2 * width + 2 * SAVED_ROWS
         blocks = [both[first + at : first + at + LANES] for at in range(0, width, LANES)]
         return across(rows, jnp.concatenate(blocks, axis=1))
 
-    rows = jnp.concatenate([part[:, :width] for part in arrived])
+    rows = arrived[:, :width]
     own, other = routed(core), routed(1 - core)
     grad_gate1, grad_up1, gates1 = backward(own, back(both1), both1)
     grad_gate2, grad_up2, gates2 = backward(other, back(both2), both2)
@@ -146,8 +140,9 @@
     step = 512 if width % 512 == 0 else LANES
     for at in range(0, width, step):
         weights = [b[first + at : first + at + step] for b in (both1, both2) for first in (0, width)]
-        store(slice(at, at + step), across(grads, jnp.concatenate(weights, axis=1)))
-    store(slice(width, width + LANES), gates1 + gates2)
+        pieces = across(grads, jnp.concatenate(weights, axis=1))
+        out[:, at : at + step] = pieces.astype(out.dtype)
+    out[:, width:] = (gates1 + gates2).astype(out.dtype)
 
 
 def stay_in(space, *arrays):
@@ -198,11 +193,12 @@
     )
     both2 = swap_cores(both)
     arrived = exchange(sent, ("row", "inner"))
+    arrived = jnp.swapaxes(arrived, 0, 1).reshape(half, packed)
     pieces = pl.pallas_call(
-        functools.partial(expert_kernel, own, topk, slots),
-        out_shape=[jax.ShapeDtypeStruct((peers, packed), bf16)] * own,
-        in_specs=[in_vmem] * (own + 2),
-        out_specs=[in_vmem] * own,
+        functools.partial(expert_kernel, topk, slots),
+        out_shape=jax.ShapeDtypeStruct((half, packed), bf16),
+        in_specs=[in_vmem] * 3,
+        out_specs=in_vmem,
         compiler_params=pltpu.CompilerParams(vmem_limit_bytes=16 * 2**20),
         cost_estimate=pl.CostEstimate(
             flops=12 * half * w_down.size,
@@ -210,11 +206,9 @@
             transcendentals=2 * half * hidden,
         ),
         name="expert_pieces",
-    )(
-        *(arrived[:, at] for at in range(own)),
-        *stay_in(pltpu.VMEM, both, both2),
-    )
-    returned = exchange(jnp.stack(pieces, axis=1), ("row", "inner"))
+    )(arrived, *stay_in(pltpu.VMEM, both, both2))
+    pieces = jnp.swapaxes(pieces.reshape(own, peers, packed), 0, 1)
+    returned = exchange(pieces, ("row", "inner"))
     rows, gates = returned[:, :, :width], returned[:, :, width : width + topk]
     grad_rows = jnp.sum(rows.astype(jnp.float32), axis=0).astype(out_grad.dtype)
     return grad_rows, jnp.sum(gates.astype(jnp.float32), axis=0)

time: 37.1 us -> 36.7 us (0.989)
  transfers between devices with their start and end apart: 1 -> 1, of which waited for: 0 -> 0; matrix products, arithmetic and copies ran while one was open for 1% -> 0% of each run, Pallas kernels for 0% -> 0%
where the time goes in v1:
time: 36.7 us; the launch traced here: 36.4 us
  blocking collectives  29.9 us (81%)
  Pallas kernels  3.72 us (10%)
  other arithmetic  1.38 us (4%)
  between operations  0.67 us (2%)
  starting transfers between devices  0.52 us (1%)
    all_to_all x2, blocking collectives, exchange(): return lax.all_to_all(array, axis, split_axis=0, concat_axis=0, tiled=True)  29.9 us
    pallas_call x1, Pallas kernels, flat(): pl.pallas_call(pack_kernel, out_shape=[jax.ShapeDtypeStruct((peers, own,...  1.99 us
    pallas_call x1, Pallas kernels, flat(): pl.pallas_call(functools.partial(expert_kernel, topk, slots), out_shape=j...  1.73 us
    reduce_sum x1, other arithmetic, flat(): grad_rows = jnp.sum(rows.astype(jnp.float32), axis=0).astype(out_grad.dtype)  0.79 us
  transfers between devices with their start and end apart: 1, of which 0 were waited for; matrix products, arithmetic and copies ran while one was open for 0% of the time, Pallas kernels for 0%

profile of v1, /device:TPU:0, one launch (start us, length us, event | category | flops | bytes accessed | tf_op | source)
XLA Modules:
  0.0 36.4 jit_solution(15487721886214314104)
XLA Ops:
  0.6 2.0 %pack_rows.1 = (bf16[16,2,3712]{2,1,0:T(2,128)(2,1)S(1)}, bf16[10816,128]{1,0:T(8,128)(2,1)S(1)}) custom-call(bf16[2,3584]{1,0:T(2,128)(2,1)} %out_grad.1, s32[2,4]{1,0:T(2,128)} %ids.1, s32[2,4]{1,0:T(2,128)} %slots.1, bf16[2,4]{1,0:T(2,128)(2,1)} %weights.1, bf16[3584,128]{1,0:T(8,128)(2,1)} %w_gate.1, bf16[3584,128]{1,0:T(8,128)(2,1)} %w_up.1, ...), custom_call_target="tpu_custom_call" | custom-call | tf_op jit(solution)/shard_map/pack_rows/pallas_call | solution.py:169
  2.6 0.5 %collective-permute-start = (bf16[10816,128]{1,0:T(8,128)(2,1)S(1)}, bf16[10816,128]{1,0:T(8,128)(2,1)S(1)}, u32[]{:S(2)}, u32[]{:S(2)}) collective-permute-start(bf16[10816,128]{1,0:T(8,128)(2,1)S(1)} %get-tuple-element.5.both1), channel_id=1, source_target_pairs={{0,8},{8,0},{1,9},{9,1},{2,10},{10,2},{3,11},{11,3},{4,12},{12,4},... | collective-permute-start | bytes 8306696 | tf_op jit(solution)/shard_map/ppermute | solution.py:153
  3.2 17.7 %all_to_all.10 = bf16[16,2,3712]{2,1,0:T(2,128)(2,1)S(1)} all-to-all(bf16[16,2,3712]{2,1,0:T(2,128)(2,1)S(1)} %get-tuple-element.4), channel_id=1, replica_groups=mesh['row'=2,'core'=2,'inner'=8] {'row','inner'}, dimensions={0} | all-to-all | bytes 475136 | tf_op jit(solution)/shard_map/all_to_all | solution.py:16
  20.9 0.0 collective-permute-done.both2
  20.9 1.7 %expert_pieces.1 = bf16[32,3712]{1,0:T(8,128)(2,1)S(1)} custom-call(bf16[32,3712]{1,0:T(8,128)(2,1)S(1)} %bitcast.6, bf16[10816,128]{1,0:T(8,128)(2,1)S(1)} %get-tuple-element.5.both1, bf16[10816,128]{1,0:T(8,128)(2,1)S(1)} %collective-permute-done.both2), custom_call_target="tpu_custom_call" | custom-call | flops 176160768 | bytes 6012928 | tf_op jit(solution)/shard_map/expert_pieces/pallas_call | solution.py:197
  22.7 0.2 copy.14
  22.9 12.2 %all_to_all.11 = bf16[16,2,3712]{2,1,0:T(2,128)(2,1)S(1)} all-to-all(bf16[16,2,3712]{2,1,0:T(2,128)(2,1)S(1)} %bitcast.9), channel_id=1, replica_groups=mesh['row'=2,'core'=2,'inner'=8] {'row','inner'}, dimensions={0} | all-to-all | bytes 475136 | tf_op jit(solution)/shard_map/all_to_all | solution.py:16
  35.1 0.6 %convert_reduce_fusion = f32[2,4]{1,0:T(2,128)} fusion(bf16[16,2,3712]{2,1,0:T(2,128)(2,1)S(1)} %all_to_all.11), kind=kLoop, calls=%fused_computation.2 | loop fusion | flops 248 | bytes 288 | tf_op jit(solution)/shard_map/reduce_sum | solution.py:214
  35.6 0.8 %slice_reduce_fusion = bf16[2,3584]{1,0:T(2,128)(2,1)} fusion(bf16[16,2,3712]{2,1,0:T(2,128)(2,1)S(1)} %all_to_all.11), kind=kLoop, calls=%fused_computation.1 | loop fusion | flops 107520 | bytes 243712 | tf_op jit(solution)/shard_map/reduce_sum | solution.py:213
  (1 shorter events, 0.0 us)
Async XLA Ops:
  2.6 18.3 %collective-permute-start = (bf16[10816,128]{1,0:T(8,128)(2,1)S(1)}, bf16[10816,128]{1,0:T(8,128)(2,1)S(1)}, u32[]{:S(2)}, u32[]{:S(2)}) collective-permute-start(bf16[10816,128]{1,0:T(8,128)(2,1)S(1)} %get-tuple-element.5.both1), channel_id=1, source_target_pairs={{0,8},{8,0},{1,9},{9,1},{2,10},{10,2},{3,11},{11,3},{4,12},{12,4},... | collective-permute-start | bytes 8306696 | tf_op jit(solution)/shard_map/ppermute | solution.py:153

commit v2 on v1

--- a/solution.py
+++ b/solution.py
@@ -10,6 +10,7 @@
 LANES = 128
 CORES = 2
 SAVED_ROWS = 32
+WEIGHT_COPIES = 4
 
 
 def exchange(array, axis):
@@ -49,6 +50,7 @@
 ):
     width, topk = w_gate.shape[0], ids.shape[1]
     first_down = 2 * width + 2 * SAVED_ROWS
+    part = width // WEIGHT_COPIES
     copies = [
         pltpu.make_async_copy(source, target, sems.at[at])
         for at, (source, target) in enumerate(
@@ -58,8 +60,11 @@
                 (weights, reals),
                 (out_grad, rows),
                 (pre_act, saved),
-                (w_gate, both.at[:width]),
-                (w_up, both.at[width : 2 * width]),
+                *(
+                    (source.at[at : at + part], both.at[first + at : first + at + part])
+                    for source, first in ((w_gate, 0), (w_up, width))
+                    for at in range(0, width, part)
+                ),
                 *(
                     (w_down.at[:, at : at + LANES], both.at[first_down + at : first_down + at + LANES])
                     for at in range(0, width, LANES)
@@ -145,6 +150,29 @@
     out[:, width:] = (gates1 + gates2).astype(out.dtype)
 
 
+def final_kernel(pieces, grad_rows, grad_gate, rows, gates, sems):
+    width, topk = rows.shape[1], gates.shape[1]
+
+    def summed(cols):
+        total = pieces[0, :, cols].astype(jnp.float32)
+        for peer in range(1, pieces.shape[0]):
+            total = total + pieces[peer, :, cols].astype(jnp.float32)
+        return total
+
+    copies = [pltpu.make_async_copy(gates, grad_gate, sems.at[0])]
+    gates[...] = summed(slice(width, width + LANES))[:, :topk]
+    copies[0].start()
+    for at in range(2):
+        cols = slice(at * width // 2, (at + 1) * width // 2)
+        rows[:, cols] = summed(cols).astype(rows.dtype)
+        copies.append(
+            pltpu.make_async_copy(rows.at[:, cols], grad_rows.at[:, cols], sems.at[1 + at])
+        )
+        copies[-1].start()
+    for copy in copies:
+        copy.wait()
+
+
 def stay_in(space, *arrays):
     return [pltpu.with_memory_space_constraint(a, space) for a in arrays]
 
@@ -180,7 +208,7 @@
             pltpu.VMEM((own, topk), bf16),
             pltpu.VMEM(pre_act.shape, bf16),
             pltpu.VMEM((own, LANES), jnp.float32),
-            pltpu.SemaphoreType.DMA((7 + width // LANES,)),
+            pltpu.SemaphoreType.DMA((5 + 2 * WEIGHT_COPIES + width // LANES,)),
         ],
         compiler_params=pltpu.CompilerParams(vmem_limit_bytes=16 * 2**20),
         name="pack_rows",
@@ -209,9 +237,22 @@
     )(arrived, *stay_in(pltpu.VMEM, both, both2))
     pieces = jnp.swapaxes(pieces.reshape(own, peers, packed), 0, 1)
     returned = exchange(pieces, ("row", "inner"))
-    rows, gates = returned[:, :, :width], returned[:, :, width : width + topk]
-    grad_rows = jnp.sum(rows.astype(jnp.float32), axis=0).astype(out_grad.dtype)
-    return grad_rows, jnp.sum(gates.astype(jnp.float32), axis=0)
+    return pl.pallas_call(
+        final_kernel,
+        out_shape=[
+            jax.ShapeDtypeStruct((own, width), bf16),
+            jax.ShapeDtypeStruct((own, topk), jnp.float32),
+        ],
+        in_specs=[in_vmem],
+        out_specs=[in_hbm] * 2,
+        scratch_shapes=[
+            pltpu.VMEM((own, width), bf16),
+            pltpu.VMEM((own, topk), jnp.float32),
+            pltpu.SemaphoreType.DMA((3,)),
+        ],
+        compiler_params=pltpu.CompilerParams(vmem_limit_bytes=16 * 2**20),
+        name="sum_pieces",
+    )(returned)
 
 
 def staged(out_grad, routing_weight, expert_ids, slot_index, w_gate, w_up, w_down, pre_act):

time: 36.7 us -> 36.1 us (0.984)
  other arithmetic: 1.38 us -> 0 us
  Pallas kernels: 3.72 us -> 4.57 us
    reduce_sum x2 -> x0, other arithmetic: 1.38 us -> none  [the longest x1 0.79 us: flat(): grad_rows = jnp.sum(rows.astype(jnp.float32), axis=0).astype(out_grad.dtype)]
    pallas_call x0 -> x1, Pallas kernels: none -> 0.68 us  [flat(): pl.pallas_call(final_kernel, out_shape=[jax.ShapeDtypeStruct((own, width)...]
where the time goes in v2:
time: 36.1 us; the launch traced here: 35.9 us
  blocking collectives  29.9 us (83%)
  Pallas kernels  4.57 us (13%)
  between operations  0.67 us (2%)
  starting transfers between devices  0.52 us (1%)
    all_to_all x2, blocking collectives, exchange(): return lax.all_to_all(array, axis, split_axis=0, concat_axis=0, tiled=True)  29.9 us
    pallas_call x1, Pallas kernels, flat(): pl.pallas_call(pack_kernel, out_shape=[jax.ShapeDtypeStruct((peers, own,...  2.16 us
    pallas_call x1, Pallas kernels, flat(): pl.pallas_call(functools.partial(expert_kernel, topk, slots), out_shape=j...  1.73 us
  transfers between devices with their start and end apart: 1, of which 0 were waited for; matrix products, arithmetic and copies ran while one was open for 0% of the time, Pallas kernels for 0%

profile of v2, /device:TPU:0, one launch (start us, length us, event | category | flops | bytes accessed | tf_op | source)
XLA Modules:
  0.0 35.9 jit_solution(16256688664028207882)
XLA Ops:
  0.6 2.2 %pack_rows.1 = (bf16[16,2,3712]{2,1,0:T(2,128)(2,1)S(1)}, bf16[10816,128]{1,0:T(8,128)(2,1)S(1)}) custom-call(bf16[2,3584]{1,0:T(2,128)(2,1)} %out_grad.1, s32[2,4]{1,0:T(2,128)} %ids.1, s32[2,4]{1,0:T(2,128)} %slots.1, bf16[2,4]{1,0:T(2,128)(2,1)} %weights.1, bf16[3584,128]{1,0:T(8,128)(2,1)} %w_gate.1, bf16[3584,128]{1,0:T(8,128)(2,1)} %w_up.1, ...), custom_call_target="tpu_custom_call" | custom-call | tf_op jit(solution)/shard_map/pack_rows/pallas_call | solution.py:197
  2.8 0.5 %collective-permute-start = (bf16[10816,128]{1,0:T(8,128)(2,1)S(1)}, bf16[10816,128]{1,0:T(8,128)(2,1)S(1)}, u32[]{:S(2)}, u32[]{:S(2)}) collective-permute-start(bf16[10816,128]{1,0:T(8,128)(2,1)S(1)} %get-tuple-element.5.both1), channel_id=1, source_target_pairs={{0,8},{8,0},{1,9},{9,1},{2,10},{10,2},{3,11},{11,3},{4,12},{12,4},... | collective-permute-start | bytes 8306696 | tf_op jit(solution)/shard_map/ppermute | solution.py:181
  3.3 17.7 %all_to_all.10 = bf16[16,2,3712]{2,1,0:T(2,128)(2,1)S(1)} all-to-all(bf16[16,2,3712]{2,1,0:T(2,128)(2,1)S(1)} %get-tuple-element.4), channel_id=1, replica_groups=mesh['row'=2,'core'=2,'inner'=8] {'row','inner'}, dimensions={0} | all-to-all | bytes 475136 | tf_op jit(solution)/shard_map/all_to_all | solution.py:17
  21.1 0.0 collective-permute-done.both2
  21.1 1.7 %expert_pieces.1 = bf16[32,3712]{1,0:T(8,128)(2,1)S(1)} custom-call(bf16[32,3712]{1,0:T(8,128)(2,1)S(1)} %bitcast.6, bf16[10816,128]{1,0:T(8,128)(2,1)S(1)} %get-tuple-element.5.both1, bf16[10816,128]{1,0:T(8,128)(2,1)S(1)} %collective-permute-done.both2), custom_call_target="tpu_custom_call" | custom-call | flops 176160768 | bytes 6012928 | tf_op jit(solution)/shard_map/expert_pieces/pallas_call | solution.py:225
  22.8 0.2 copy.14
  23.0 12.2 %all_to_all.11.pieces = bf16[16,2,3712]{2,1,0:T(2,128)(2,1)S(1)} all-to-all(bf16[16,2,3712]{2,1,0:T(2,128)(2,1)S(1)} %bitcast.9), channel_id=1, replica_groups=mesh['row'=2,'core'=2,'inner'=8] {'row','inner'}, dimensions={0} | all-to-all | bytes 475136 | tf_op jit(solution)/shard_map/all_to_all | solution.py:17
  35.2 0.7 %sum_pieces.1 = (bf16[2,3584]{1,0:T(2,128)(2,1)}, f32[2,4]{1,0:T(2,128)}) custom-call(bf16[16,2,3712]{2,1,0:T(2,128)(2,1)S(1)} %all_to_all.11.pieces), custom_call_target="tpu_custom_call" | custom-call | tf_op jit(solution)/shard_map/sum_pieces/pallas_call | solution.py:240
  (1 shorter events, 0.0 us)
Async XLA Ops:
  2.8 18.3 %collective-permute-start = (bf16[10816,128]{1,0:T(8,128)(2,1)S(1)}, bf16[10816,128]{1,0:T(8,128)(2,1)S(1)}, u32[]{:S(2)}, u32[]{:S(2)}) collective-permute-start(bf16[10816,128]{1,0:T(8,128)(2,1)S(1)} %get-tuple-element.5.both1), channel_id=1, source_target_pairs={{0,8},{8,0},{1,9},{9,1},{2,10},{10,2},{3,11},{11,3},{4,12},{12,4},... | collective-permute-start | bytes 8306696 | tf_op jit(solution)/shard_map/ppermute | solution.py:181

commit v3 on v2

--- a/solution.py
+++ b/solution.py
@@ -10,7 +10,6 @@
 LANES = 128
 CORES = 2
 SAVED_ROWS = 32
-WEIGHT_COPIES = 4
 
 
 def exchange(array, axis):
@@ -50,7 +49,6 @@
 ):
     width, topk = w_gate.shape[0], ids.shape[1]
     first_down = 2 * width + 2 * SAVED_ROWS
-    part = width // WEIGHT_COPIES
     copies = [
         pltpu.make_async_copy(source, target, sems.at[at])
         for at, (source, target) in enumerate(
@@ -60,11 +58,8 @@
                 (weights, reals),
                 (out_grad, rows),
                 (pre_act, saved),
-                *(
-                    (source.at[at : at + part], both.at[first + at : first + at + part])
-                    for source, first in ((w_gate, 0), (w_up, width))
-                    for at in range(0, width, part)
-                ),
+                (w_gate, both.at[:width]),
+                (w_up, both.at[width : 2 * width]),
                 *(
                     (w_down.at[:, at : at + LANES], both.at[first_down + at : first_down + at + LANES])
                     for at in range(0, width, LANES)
@@ -141,12 +136,17 @@
     own, other = routed(core), routed(1 - core)
     grad_gate1, grad_up1, gates1 = backward(own, back(both1), both1)
     grad_gate2, grad_up2, gates2 = backward(other, back(both2), both2)
-    grads = jnp.concatenate([grad_gate1, grad_up1, grad_gate2, grad_up2], axis=1)
+    grads1 = jnp.concatenate([grad_gate1, grad_up1], axis=1)
+    grads2 = jnp.concatenate([grad_gate2, grad_up2], axis=1)
+
+    def pieces(grads, both, at):
+        weights = [both[first + at : first + at + step] for first in (0, width)]
+        return across(grads, jnp.concatenate(weights, axis=1))
+
     step = 512 if width % 512 == 0 else LANES
     for at in range(0, width, step):
-        weights = [b[first + at : first + at + step] for b in (both1, both2) for first in (0, width)]
-        pieces = across(grads, jnp.concatenate(weights, axis=1))
-        out[:, at : at + step] = pieces.astype(out.dtype)
+        total = pieces(grads1, both1, at) + pieces(grads2, both2, at)
+        out[:, at : at + step] = total.astype(out.dtype)
     out[:, width:] = (gates1 + gates2).astype(out.dtype)
 
 
@@ -208,7 +208,7 @@
             pltpu.VMEM((own, topk), bf16),
             pltpu.VMEM(pre_act.shape, bf16),
             pltpu.VMEM((own, LANES), jnp.float32),
-            pltpu.SemaphoreType.DMA((5 + 2 * WEIGHT_COPIES + width // LANES,)),
+            pltpu.SemaphoreType.DMA((7 + width // LANES,)),
         ],
         compiler_params=pltpu.CompilerParams(vmem_limit_bytes=16 * 2**20),
         name="pack_rows",

time: 36.1 us -> 36.1 us (level)
  no operation moved by 1% of the time
where the time goes in v3:
time: 36.1 us; the launch traced here: 35.9 us
  blocking collectives  29.9 us (83%)
  Pallas kernels  4.54 us (13%)
  between operations  0.66 us (2%)
  starting transfers between devices  0.52 us (1%)
    all_to_all x2, blocking collectives, exchange(): return lax.all_to_all(array, axis, split_axis=0, concat_axis=0, tiled=True)  29.9 us
    pallas_call x1, Pallas kernels, flat(): pl.pallas_call(pack_kernel, out_shape=[jax.ShapeDtypeStruct((peers, own,...  1.99 us
    pallas_call x1, Pallas kernels, flat(): pl.pallas_call(functools.partial(expert_kernel, topk, slots), out_shape=j...  1.86 us
  transfers between devices with their start and end apart: 1, of which 0 were waited for; matrix products, arithmetic and copies ran while one was open for 0% of the time, Pallas kernels for 0%

profile of v3, /device:TPU:0, one launch (start us, length us, event | category | flops | bytes accessed | tf_op | source)
XLA Modules:
  0.0 35.9 jit_solution(11010709460794524417)
XLA Ops:
  0.6 2.0 %pack_rows.1 = (bf16[16,2,3712]{2,1,0:T(2,128)(2,1)S(1)}, bf16[10816,128]{1,0:T(8,128)(2,1)S(1)}) custom-call(bf16[2,3584]{1,0:T(2,128)(2,1)} %out_grad.1, s32[2,4]{1,0:T(2,128)} %ids.1, s32[2,4]{1,0:T(2,128)} %slots.1, bf16[2,4]{1,0:T(2,128)(2,1)} %weights.1, bf16[3584,128]{1,0:T(8,128)(2,1)} %w_gate.1, bf16[3584,128]{1,0:T(8,128)(2,1)} %w_up.1, ...), custom_call_target="tpu_custom_call" | custom-call | tf_op jit(solution)/shard_map/pack_rows/pallas_call | solution.py:197
  2.6 0.5 %collective-permute-start = (bf16[10816,128]{1,0:T(8,128)(2,1)S(1)}, bf16[10816,128]{1,0:T(8,128)(2,1)S(1)}, u32[]{:S(2)}, u32[]{:S(2)}) collective-permute-start(bf16[10816,128]{1,0:T(8,128)(2,1)S(1)} %get-tuple-element.5.both1), channel_id=1, source_target_pairs={{0,8},{8,0},{1,9},{9,1},{2,10},{10,2},{3,11},{11,3},{4,12},{12,4},... | collective-permute-start | bytes 8306696 | tf_op jit(solution)/shard_map/ppermute | solution.py:181
  3.2 17.7 %all_to_all.10 = bf16[16,2,3712]{2,1,0:T(2,128)(2,1)S(1)} all-to-all(bf16[16,2,3712]{2,1,0:T(2,128)(2,1)S(1)} %get-tuple-element.4), channel_id=1, replica_groups=mesh['row'=2,'core'=2,'inner'=8] {'row','inner'}, dimensions={0} | all-to-all | bytes 475136 | tf_op jit(solution)/shard_map/all_to_all | solution.py:16
  20.9 0.0 collective-permute-done.both2
  20.9 1.9 %expert_pieces.1 = bf16[32,3712]{1,0:T(8,128)(2,1)S(1)} custom-call(bf16[32,3712]{1,0:T(8,128)(2,1)S(1)} %bitcast.6, bf16[10816,128]{1,0:T(8,128)(2,1)S(1)} %get-tuple-element.5.both1, bf16[10816,128]{1,0:T(8,128)(2,1)S(1)} %collective-permute-done.both2), custom_call_target="tpu_custom_call" | custom-call | flops 176160768 | bytes 6012928 | tf_op jit(solution)/shard_map/expert_pieces/pallas_call | solution.py:225
  22.8 0.2 copy.14
  23.0 12.2 %all_to_all.11.pieces = bf16[16,2,3712]{2,1,0:T(2,128)(2,1)S(1)} all-to-all(bf16[16,2,3712]{2,1,0:T(2,128)(2,1)S(1)} %bitcast.9), channel_id=1, replica_groups=mesh['row'=2,'core'=2,'inner'=8] {'row','inner'}, dimensions={0} | all-to-all | bytes 475136 | tf_op jit(solution)/shard_map/all_to_all | solution.py:16
  35.2 0.7 %sum_pieces.1 = (bf16[2,3584]{1,0:T(2,128)(2,1)}, f32[2,4]{1,0:T(2,128)}) custom-call(bf16[16,2,3712]{2,1,0:T(2,128)(2,1)S(1)} %all_to_all.11.pieces), custom_call_target="tpu_custom_call" | custom-call | tf_op jit(solution)/shard_map/sum_pieces/pallas_call | solution.py:240
  (1 shorter events, 0.0 us)
Async XLA Ops:
  2.6 18.3 %collective-permute-start = (bf16[10816,128]{1,0:T(8,128)(2,1)S(1)}, bf16[10816,128]{1,0:T(8,128)(2,1)S(1)}, u32[]{:S(2)}, u32[]{:S(2)}) collective-permute-start(bf16[10816,128]{1,0:T(8,128)(2,1)S(1)} %get-tuple-element.5.both1), channel_id=1, source_target_pairs={{0,8},{8,0},{1,9},{9,1},{2,10},{10,2},{3,11},{11,3},{4,12},{12,4},... | collective-permute-start | bytes 8306696 | tf_op jit(solution)/shard_map/ppermute | solution.py:181

commit v4 on v3

--- a/solution.py
+++ b/solution.py
@@ -136,17 +136,12 @@
     own, other = routed(core), routed(1 - core)
     grad_gate1, grad_up1, gates1 = backward(own, back(both1), both1)
     grad_gate2, grad_up2, gates2 = backward(other, back(both2), both2)
-    grads1 = jnp.concatenate([grad_gate1, grad_up1], axis=1)
-    grads2 = jnp.concatenate([grad_gate2, grad_up2], axis=1)
-
-    def pieces(grads, both, at):
-        weights = [both[first + at : first + at + step] for first in (0, width)]
-        return across(grads, jnp.concatenate(weights, axis=1))
-
-    step = 512 if width % 512 == 0 else LANES
+    grads = jnp.concatenate([grad_gate1, grad_up1, grad_gate2, grad_up2], axis=1)
+    step = width // 4
     for at in range(0, width, step):
-        total = pieces(grads1, both1, at) + pieces(grads2, both2, at)
-        out[:, at : at + step] = total.astype(out.dtype)
+        weights = [b[first + at : first + at + step] for b in (both1, both2) for first in (0, width)]
+        pieces = across(grads, jnp.concatenate(weights, axis=1))
+        out[:, at : at + step] = pieces.astype(out.dtype)
     out[:, width:] = (gates1 + gates2).astype(out.dtype)
 
 

time: 36.1 us -> 36 us (level)
  no operation moved by 1% of the time
where the time goes in v4:
time: 36 us; the launch traced here: 35.7 us
  blocking collectives  29.9 us (83%)
  Pallas kernels  4.4 us (12%)
  between operations  0.67 us (2%)
  starting transfers between devices  0.52 us (1%)
    all_to_all x2, blocking collectives, exchange(): return lax.all_to_all(array, axis, split_axis=0, concat_axis=0, tiled=True)  29.9 us
    pallas_call x1, Pallas kernels, flat(): pl.pallas_call(pack_kernel, out_shape=[jax.ShapeDtypeStruct((peers, own,...  1.99 us
    pallas_call x1, Pallas kernels, flat(): pl.pallas_call(functools.partial(expert_kernel, topk, slots), out_shape=j...  1.73 us
  transfers between devices with their start and end apart: 1, of which 0 were waited for; matrix products, arithmetic and copies ran while one was open for 0% of the time, Pallas kernels for 0%

profile of v4, /device:TPU:0, one launch (start us, length us, event | category | flops | bytes accessed | tf_op | source)
XLA Modules:
  0.0 35.7 jit_solution(1590142993004423587)
XLA Ops:
  0.6 2.0 %pack_rows.1 = (bf16[16,2,3712]{2,1,0:T(2,128)(2,1)S(1)}, bf16[10816,128]{1,0:T(8,128)(2,1)S(1)}) custom-call(bf16[2,3584]{1,0:T(2,128)(2,1)} %out_grad.1, s32[2,4]{1,0:T(2,128)} %ids.1, s32[2,4]{1,0:T(2,128)} %slots.1, bf16[2,4]{1,0:T(2,128)(2,1)} %weights.1, bf16[3584,128]{1,0:T(8,128)(2,1)} %w_gate.1, bf16[3584,128]{1,0:T(8,128)(2,1)} %w_up.1, ...), custom_call_target="tpu_custom_call" | custom-call | tf_op jit(solution)/shard_map/pack_rows/pallas_call | solution.py:192
  2.6 0.5 %collective-permute-start = (bf16[10816,128]{1,0:T(8,128)(2,1)S(1)}, bf16[10816,128]{1,0:T(8,128)(2,1)S(1)}, u32[]{:S(2)}, u32[]{:S(2)}) collective-permute-start(bf16[10816,128]{1,0:T(8,128)(2,1)S(1)} %get-tuple-element.5.both1), channel_id=1, source_target_pairs={{0,8},{8,0},{1,9},{9,1},{2,10},{10,2},{3,11},{11,3},{4,12},{12,4},... | collective-permute-start | bytes 8306696 | tf_op jit(solution)/shard_map/ppermute | solution.py:176
  3.2 17.7 %all_to_all.10 = bf16[16,2,3712]{2,1,0:T(2,128)(2,1)S(1)} all-to-all(bf16[16,2,3712]{2,1,0:T(2,128)(2,1)S(1)} %get-tuple-element.4), channel_id=1, replica_groups=mesh['row'=2,'core'=2,'inner'=8] {'row','inner'}, dimensions={0} | all-to-all | bytes 475136 | tf_op jit(solution)/shard_map/all_to_all | solution.py:16
  20.9 0.0 collective-permute-done.both2
  20.9 1.7 %expert_pieces.1 = bf16[32,3712]{1,0:T(8,128)(2,1)S(1)} custom-call(bf16[32,3712]{1,0:T(8,128)(2,1)S(1)} %bitcast.6, bf16[10816,128]{1,0:T(8,128)(2,1)S(1)} %get-tuple-element.5.both1, bf16[10816,128]{1,0:T(8,128)(2,1)S(1)} %collective-permute-done.both2), custom_call_target="tpu_custom_call" | custom-call | flops 176160768 | bytes 6012928 | tf_op jit(solution)/shard_map/expert_pieces/pallas_call | solution.py:220
  22.7 0.2 copy.14
  22.9 12.2 %all_to_all.11.pieces = bf16[16,2,3712]{2,1,0:T(2,128)(2,1)S(1)} all-to-all(bf16[16,2,3712]{2,1,0:T(2,128)(2,1)S(1)} %bitcast.9), channel_id=1, replica_groups=mesh['row'=2,'core'=2,'inner'=8] {'row','inner'}, dimensions={0} | all-to-all | bytes 475136 | tf_op jit(solution)/shard_map/all_to_all | solution.py:16
  35.1 0.7 %sum_pieces.1 = (bf16[2,3584]{1,0:T(2,128)(2,1)}, f32[2,4]{1,0:T(2,128)}) custom-call(bf16[16,2,3712]{2,1,0:T(2,128)(2,1)S(1)} %all_to_all.11.pieces), custom_call_target="tpu_custom_call" | custom-call | tf_op jit(solution)/shard_map/sum_pieces/pallas_call | solution.py:235
  (1 shorter events, 0.0 us)
Async XLA Ops:
  2.6 18.3 %collective-permute-start = (bf16[10816,128]{1,0:T(8,128)(2,1)S(1)}, bf16[10816,128]{1,0:T(8,128)(2,1)S(1)}, u32[]{:S(2)}, u32[]{:S(2)}) collective-permute-start(bf16[10816,128]{1,0:T(8,128)(2,1)S(1)} %get-tuple-element.5.both1), channel_id=1, source_target_pairs={{0,8},{8,0},{1,9},{9,1},{2,10},{10,2},{3,11},{11,3},{4,12},{12,4},... | collective-permute-start | bytes 8306696 | tf_op jit(solution)/shard_map/ppermute | solution.py:176

commit v5 on v4

--- a/solution.py
+++ b/solution.py
@@ -154,16 +154,14 @@
             total = total + pieces[peer, :, cols].astype(jnp.float32)
         return total
 
-    copies = [pltpu.make_async_copy(gates, grad_gate, sems.at[0])]
+    copies = [
+        pltpu.make_async_copy(gates, grad_gate, sems.at[0]),
+        pltpu.make_async_copy(rows, grad_rows, sems.at[1]),
+    ]
     gates[...] = summed(slice(width, width + LANES))[:, :topk]
     copies[0].start()
-    for at in range(2):
-        cols = slice(at * width // 2, (at + 1) * width // 2)
-        rows[:, cols] = summed(cols).astype(rows.dtype)
-        copies.append(
-            pltpu.make_async_copy(rows.at[:, cols], grad_rows.at[:, cols], sems.at[1 + at])
-        )
-        copies[-1].start()
+    rows[...] = summed(slice(0, width)).astype(rows.dtype)
+    copies[1].start()
     for copy in copies:
         copy.wait()
 
@@ -243,7 +241,7 @@
         scratch_shapes=[
             pltpu.VMEM((own, width), bf16),
             pltpu.VMEM((own, topk), jnp.float32),
-            pltpu.SemaphoreType.DMA((3,)),
+            pltpu.SemaphoreType.DMA((2,)),
         ],
         compiler_params=pltpu.CompilerParams(vmem_limit_bytes=16 * 2**20),
         name="sum_pieces",

time: 36 us -> 36 us (level)
  no operation moved by 1% of the time
where the time goes in v5:
time: 36 us; the launch traced here: 35.7 us
  blocking collectives  29.9 us (83%)
  Pallas kernels  4.4 us (12%)
  between operations  0.67 us (2%)
  starting transfers between devices  0.52 us (1%)
    all_to_all x2, blocking collectives, exchange(): return lax.all_to_all(array, axis, split_axis=0, concat_axis=0, tiled=True)  29.9 us
    pallas_call x1, Pallas kernels, flat(): pl.pallas_call(pack_kernel, out_shape=[jax.ShapeDtypeStruct((peers, own,...  1.99 us
    pallas_call x1, Pallas kernels, flat(): pl.pallas_call(functools.partial(expert_kernel, topk, slots), out_shape=j...  1.73 us
  transfers between devices with their start and end apart: 1, of which 0 were waited for; matrix products, arithmetic and copies ran while one was open for 0% of the time, Pallas kernels for 0%

profile of v5, /device:TPU:0, one launch (start us, length us, event | category | flops | bytes accessed | tf_op | source)
XLA Modules:
  0.0 35.7 jit_solution(3454802145829432893)
XLA Ops:
  0.6 2.0 %pack_rows.1 = (bf16[16,2,3712]{2,1,0:T(2,128)(2,1)S(1)}, bf16[10816,128]{1,0:T(8,128)(2,1)S(1)}) custom-call(bf16[2,3584]{1,0:T(2,128)(2,1)} %out_grad.1, s32[2,4]{1,0:T(2,128)} %ids.1, s32[2,4]{1,0:T(2,128)} %slots.1, bf16[2,4]{1,0:T(2,128)(2,1)} %weights.1, bf16[3584,128]{1,0:T(8,128)(2,1)} %w_gate.1, bf16[3584,128]{1,0:T(8,128)(2,1)} %w_up.1, ...), custom_call_target="tpu_custom_call" | custom-call | tf_op jit(solution)/shard_map/pack_rows/pallas_call | solution.py:190
  2.6 0.5 %collective-permute-start = (bf16[10816,128]{1,0:T(8,128)(2,1)S(1)}, bf16[10816,128]{1,0:T(8,128)(2,1)S(1)}, u32[]{:S(2)}, u32[]{:S(2)}) collective-permute-start(bf16[10816,128]{1,0:T(8,128)(2,1)S(1)} %get-tuple-element.5.both1), channel_id=1, source_target_pairs={{0,8},{8,0},{1,9},{9,1},{2,10},{10,2},{3,11},{11,3},{4,12},{12,4},... | collective-permute-start | bytes 8306696 | tf_op jit(solution)/shard_map/ppermute | solution.py:174
  3.2 17.7 %all_to_all.10 = bf16[16,2,3712]{2,1,0:T(2,128)(2,1)S(1)} all-to-all(bf16[16,2,3712]{2,1,0:T(2,128)(2,1)S(1)} %get-tuple-element.4), channel_id=1, replica_groups=mesh['row'=2,'core'=2,'inner'=8] {'row','inner'}, dimensions={0} | all-to-all | bytes 475136 | tf_op jit(solution)/shard_map/all_to_all | solution.py:16
  20.9 0.0 collective-permute-done.both2
  20.9 1.7 %expert_pieces.1 = bf16[32,3712]{1,0:T(8,128)(2,1)S(1)} custom-call(bf16[32,3712]{1,0:T(8,128)(2,1)S(1)} %bitcast.6, bf16[10816,128]{1,0:T(8,128)(2,1)S(1)} %get-tuple-element.5.both1, bf16[10816,128]{1,0:T(8,128)(2,1)S(1)} %collective-permute-done.both2), custom_call_target="tpu_custom_call" | custom-call | flops 176160768 | bytes 6012928 | tf_op jit(solution)/shard_map/expert_pieces/pallas_call | solution.py:218
  22.7 0.2 copy.14
  22.9 12.2 %all_to_all.11.pieces = bf16[16,2,3712]{2,1,0:T(2,128)(2,1)S(1)} all-to-all(bf16[16,2,3712]{2,1,0:T(2,128)(2,1)S(1)} %bitcast.9), channel_id=1, replica_groups=mesh['row'=2,'core'=2,'inner'=8] {'row','inner'}, dimensions={0} | all-to-all | bytes 475136 | tf_op jit(solution)/shard_map/all_to_all | solution.py:16
  35.1 0.7 %sum_pieces.1 = (bf16[2,3584]{1,0:T(2,128)(2,1)}, f32[2,4]{1,0:T(2,128)}) custom-call(bf16[16,2,3712]{2,1,0:T(2,128)(2,1)S(1)} %all_to_all.11.pieces), custom_call_target="tpu_custom_call" | custom-call | tf_op jit(solution)/shard_map/sum_pieces/pallas_call | solution.py:233
  (1 shorter events, 0.0 us)
Async XLA Ops:
  2.6 18.3 %collective-permute-start = (bf16[10816,128]{1,0:T(8,128)(2,1)S(1)}, bf16[10816,128]{1,0:T(8,128)(2,1)S(1)}, u32[]{:S(2)}, u32[]{:S(2)}) collective-permute-start(bf16[10816,128]{1,0:T(8,128)(2,1)S(1)} %get-tuple-element.5.both1), channel_id=1, source_target_pairs={{0,8},{8,0},{1,9},{9,1},{2,10},{10,2},{3,11},{11,3},{4,12},{12,4},... | collective-permute-start | bytes 8306696 | tf_op jit(solution)/shard_map/ppermute | solution.py:174
